TPU v7x, 32 devices: a whole 2x2x4 slice. The times are simulated.
32 devices in a mesh: row: 4 (over y, x), col: 8 (over z, core).
Axes of the slice: x: 2, y: 2, z: 4, core: 2. Of those that a mesh axis runs over, the one named last changes fastest.
Arguments:
- trail: bfloat16 [1024, 24576], P('row', 'col'), may hold values from -6 to 6
- trail_rows: int32 [16, 192], P('row', 'col'), may hold values from 0 to 47, as said below
- owner_x: bfloat16 [16384, 1024], P(('row', 'col')), may hold values from -0.1875 to 0.1875
- owner_y: bfloat16 [16384, 1024], P(('row', 'col')), may hold values from -6 to 6
- owner_of: int32 [192], replicated, may hold values from 0 to 7, as said below
- inv_first: bfloat16 [2, 256, 256], replicated, may hold values from -0.25 to 0.25
- inv_second: bfloat16 [2, 256, 256], replicated, may hold values from -0.25 to 0.25
- couple_right: bfloat16 [2, 256, 256], replicated, may hold values from -0.25 to 0.25
- couple_left: bfloat16 [2, 256, 256], replicated, may hold values from -0.25 to 0.25
Outputs:
- updated_trail: bfloat16 [1024, 24576], P('row', 'col')
Inputs may be any that keep to these rules, and one draw needn't show every extreme that they name: `trail_rows`: for each grid row and each block column, the 4 entries in rows r * 4 to r * 4 + 3 are distinct local block rows. `owner_of`: the 6 blocks r * 48 + c * 6 + k (k < 6) have distinct owners; one owner holds at most 8 blocks of its grid row, and some owner of every grid row holds exactly 8.
All inputs are finite; a program needn't handle non-finite values.
Results may differ from a plain program's by a relative error of at most 0.0062.
Values may be sent and summed in bfloat16 or wider, within the bound.
A program may use at most 128 MiB of HBM per device.

v0:
```python
import jax
import jax.numpy as jnp
from jax import lax
from jax.sharding import PartitionSpec as P

BS = 64
PANEL = 256
PER = 6


def real_form(pair):
    top_rows = jnp.concatenate([pair[0], pair[1]], axis=1)
    low_rows = jnp.concatenate([-pair[1], pair[0]], axis=1)
    return jnp.concatenate([top_rows, low_rows], axis=0)


def halves(matrix):
    first_half = jnp.concatenate([matrix[:, :PANEL], matrix[:, 2 * PANEL : 3 * PANEL]], axis=1)
    second_half = jnp.concatenate([matrix[:, PANEL : 2 * PANEL], matrix[:, 3 * PANEL :]], axis=1)
    return (first_half, second_half)


def join_panels(left_part, right_part):
    return jnp.concatenate(
        [left_part[:, :PANEL], right_part[:, :PANEL], left_part[:, PANEL:], right_part[:, PANEL:]],
        axis=1,
    )


def form_rows(matrix, inv_first, inv_second, couple_right):
    first_half, second_half = halves(matrix)
    low_first = jnp.dot(
        first_half, real_form(inv_first), preferred_element_type=jnp.float32
    ).astype(jnp.bfloat16)
    remainder = second_half.astype(jnp.float32) - jnp.dot(
        low_first, real_form(couple_right), preferred_element_type=jnp.float32
    )
    remainder = remainder.astype(jnp.bfloat16)
    low_second = jnp.dot(
        remainder, real_form(inv_second), preferred_element_type=jnp.float32
    ).astype(jnp.bfloat16)
    return join_panels(low_first, low_second)


def form_cols(matrix, inv_first, couple_left):
    coupling = jnp.dot(
        jnp.concatenate([couple_left[0], couple_left[1]], axis=1),
        real_form(inv_first),
        preferred_element_type=jnp.float32,
    ).astype(jnp.bfloat16)
    transposed = jnp.stack([coupling[:, :PANEL].T, coupling[:, PANEL:].T])
    first_half, second_half = halves(matrix)
    remainder = second_half.astype(jnp.float32) - jnp.dot(
        first_half, real_form(transposed), preferred_element_type=jnp.float32
    )
    return join_panels(first_half, remainder.astype(jnp.bfloat16))


def stack_cols(upper_rows):
    count = upper_rows.shape[0] // BS
    real_part = upper_rows[:, : 2 * PANEL]
    imag_part = upper_rows[:, 2 * PANEL :]
    top_rows = jnp.concatenate([real_part, -imag_part], axis=1).reshape(count, BS, 4 * PANEL)
    low_rows = jnp.concatenate([imag_part, real_part], axis=1).reshape(count, BS, 4 * PANEL)
    return jnp.concatenate([top_rows, low_rows], axis=1)


def local(
    trail, trail_rows, owner_x, owner_y, owner_of, inv_first, inv_second, couple_right, couple_left
):
    col_count = lax.axis_size("col")
    my_row = lax.axis_index("row")
    my_col = lax.axis_index("col")
    row_width = 4 * PANEL
    row_blocks = PER * col_count
    owners = lax.dynamic_slice_in_dim(owner_of, my_row * row_blocks, row_blocks)
    owner_marks = (owners[:, None] == jnp.arange(col_count, dtype=jnp.int32)[None, :]).astype(
        jnp.int32
    )
    before = jnp.cumsum(owner_marks, axis=0, dtype=jnp.int32) - owner_marks
    slot_index = jnp.sum(before * owner_marks, axis=1, dtype=jnp.int32).reshape(col_count, PER)
    owner_grid = owners.reshape(col_count, PER)
    my_marks = (owner_grid == my_col).astype(jnp.int32)
    send_slots = jnp.sum(my_marks * slot_index, axis=1, dtype=jnp.int32)
    held_x = owner_x.reshape(-1, BS, row_width)
    held_y = owner_y.reshape(-1, BS, row_width)
    got_x, got_y = (
        lax.all_to_all(held_x[send_slots], "col", split_axis=0, concat_axis=0, tiled=True),
        lax.all_to_all(held_y[send_slots], "col", split_axis=0, concat_axis=0, tiled=True),
    )
    sources = lax.dynamic_index_in_dim(owner_grid, my_col, 0, keepdims=False)
    own_x = got_x[sources].reshape(PER * BS, row_width)
    own_y = got_y[sources].reshape(PER * BS, row_width)
    lower_rows = form_rows(
        lax.all_gather(own_x, "col", axis=0, tiled=True), inv_first, inv_second, couple_right
    )
    upper_rows = form_cols(lax.all_gather(own_y, "row", axis=0, tiled=True), inv_first, couple_left)
    stacked = stack_cols(upper_rows)
    column_count = stacked.shape[0]
    lower_blocks = lower_rows.reshape(-1, BS, row_width)
    trail_tiles = trail.reshape(-1, BS, column_count, 2 * BS)

    def one_slot(inputs):
        block_tile, pattern_rows = inputs
        picked = lower_blocks[pattern_rows]
        change = jnp.einsum("jbp,jqp->bjq", picked, stacked, preferred_element_type=jnp.float32)
        return (block_tile.astype(jnp.float32) - change).astype(jnp.bfloat16)

    updated = lax.map(one_slot, (trail_tiles, trail_rows))
    return updated.reshape(trail.shape)


def solution(mesh):
    placed = (
        P("row", "col"),
        P("row", "col"),
        P(("row", "col"), None),
        P(("row", "col"), None),
        P(),
        P(),
        P(),
        P(),
        P(),
    )
    return jax.shard_map(
        local, mesh=mesh, in_specs=placed, out_specs=P("row", "col"), check_vma=False
    )
```

profile of v0, /device:TPU:1, one launch (start us, length us, event | category | flops | bytes accessed | tf_op | source)
XLA Modules:
  0.0 239.1 jit_solution(10763192760506426968)
XLA Ops:
  8.0 1.6 gather_fusion.3
  9.6 6.4 %all-to-all-start.1 = ((bf16[8,64,1024]{2,1,0:T(8,128)(2,1)}), bf16[8,64,1024]{2,1,0:T(8,128)(2,1)S(1)}, u32[]{:S(2)}, u32[]{:S(2)}) async-start(bf16[8,64,1024]{2,1,0:T(8,128)(2,1)} %gather_fusion.3), calls=%async_computation.1 | async-start | bytes 2097152 | tf_op jit(solution)/shard_map/all_to_all | solution.py:89
  16.0 25.7 %all-to-all-done.1 = bf16[8,64,1024]{2,1,0:T(8,128)(2,1)S(1)} async-done(((bf16[8,64,1024]{2,1,0:T(8,128)(2,1)}), bf16[8,64,1024]{2,1,0:T(8,128)(2,1)S(1)}, u32[]{:S(2)}, u32[]{:S(2)}) %all-to-all-start.1) | async-done | bytes 1048608 | tf_op jit(solution)/shard_map/all_to_all | solution.py:89
  41.7 1.5 gather_fusion.4
  44.0 28.9 %all_to_all.10 = bf16[8,64,1024]{2,1,0:T(8,128)(2,1)S(1)} all-to-all(bf16[8,64,1024]{2,1,0:T(8,128)(2,1)S(1)} %gather_fusion.1), channel_id=1, replica_groups=mesh['row'=4,'col'=8] {'col'}, dimensions={0} | all-to-all | bytes 2097152 | tf_op jit(solution)/shard_map/all_to_all | solution.py:88
  72.8 1.6 gather_fusion.2
  74.5 2.9 %copy.18 = bf16[32,8,24,128]{3,2,1,0:T(8,128)(2,1)} copy(bf16[32,8,24,128]{3,1,2,0:T(8,128)(2,1)} %bitcast.102) | data formatting | bytes 3145728
  78.7 7.8 %all-gather.5.cloned.1.call-done = bf16[1536,1024]{1,0:T(8,128)(2,1)} async-done(((bf16[384,1024]{1,0:T(8,128)(2,1)}), bf16[1536,1024]{1,0:T(8,128)(2,1)}) %all-gather.5.cloned.1.call-update) | async-done | bytes 3145744 | tf_op jit(solution)/shard_map/all_gather | solution.py:97
  86.5 2.1 fusion.54
  90.7 3.1 %pad_maximum_fusion.1 = bf16[24,128,1024]{2,1,0:T(8,128)(2,1)} fusion(bf16[24,64,1024]{2,1,0:T(8,128)(2,1)S(1)} %bitcast.95, bf16[24,64,512]{2,1,0:T(8,128)(2,1)S(1)} %maximum_negate_fusion, bf16[24,64,512]{2,1,0:T(8,128)(2,1)S(1)} %bitcast.99), kind=kLoop, calls=%fused_computation.18 | loop fusion | flops 18874368 | bytes 12582912 | tf_op jit(solution)/shard_map/concatenate | solution.py:65
  93.8 59.5 %all-gather.3.cloned.1.call-done = bf16[3072,1024]{1,0:T(8,128)(2,1)} async-done(((bf16[384,1024]{1,0:T(8,128)(2,1)}), bf16[3072,1024]{1,0:T(8,128)(2,1)}) %all-gather.3.cloned.1.call-update) | async-done | bytes 6291472 | tf_op jit(solution)/shard_map/all_gather | solution.py:95
  153.3 4.9 %fusion.53 = (bf16[3072,256]{1,0:T(8,128)(2,1)}, bf16[3072,256]{1,0:T(8,128)(2,1)}, bf16[3072,256]{1,0:T(8,128)(2,1)S(1)}, bf16[3072,256]{1,0:T(8,128)(2,1)S(1)}) fusion(bf16[3072,1024]{1,0:T(8,128)(2,1)} %all-gather.3.cloned.1.call-done), kind=kLoop, calls=%fused_computation.87 | loop fusion | bytes 12582912 | tf_op jit(solution)/shard_map/slice | solution.py:19
  158.3 1.9 convolution_convert_fusion.1
  160.4 1.5 copy-done.2
  161.9 8.1 %convolution_convert_fusion = bf16[3072,512]{0,1:T(8,128)(2,1)} fusion(bf16[3072,512]{0,1:T(8,128)(2,1)} %copy-done.2, bf16[3072,256]{1,0:T(8,128)(2,1)} %get-tuple-element.63, bf16[3072,256]{1,0:T(8,128)(2,1)} %get-tuple-element.62, bf16[256,256]{1,0:T(8,128)(2,1)} %get-tuple-element.86, bf16[256,256]{1,0:T(8,128)(2,1)S(1)} %get-tuple-element.88, ...), kind=kOutput, calls=%fused_computation.20 | convolution fusion | flops 3236429824 | bytes 10223616 | tf_op jit(solution)/shard_map/dot_general | solution.py:39
  170.0 2.1 fusion.56
  172.1 3.2 %pad_maximum_fusion = bf16[3072,1024]{0,1:T(8,128)(2,1)} fusion(bf16[3072,256]{0,1:T(8,128)(2,1)S(1)} %get-tuple-element.73, bf16[3072,256]{0,1:T(8,128)(2,1)S(1)} %get-tuple-element.71, bf16[3072,256]{0,1:T(8,128)(2,1)S(1)} %get-tuple-element.72, bf16[3072,256]{0,1:T(8,128)(2,1)S(1)} %get-tuple-element.70), kind=kLoop, calls=%fused_computation.17 | loop fusion | flops 25165824 | bytes 12582912 | tf_op jit(solution)/shard_map/concatenate | solution.py:24
  175.3 8.6 %copy.12 = bf16[3072,1024]{1,0:T(8,128)(2,1)} copy(bf16[3072,1024]{0,1:T(8,128)(2,1)} %pad_maximum_fusion) | data formatting | bytes 12582912 | tf_op jit(solution)/shard_map/concatenate | solution.py:24
  183.9 45.4 %while.10 = (s32[]{:T(128)}, bf16[4,64,24,128]{3,2,1,0:T(8,128)(2,1)}, bf16[4,64,24,128]{3,2,1,0:T(8,128)(2,1)}, s32[4,24]{1,0:T(4,128)}, bf16[48,64,1024]{2,1,0...) while((s32[]{:T(128)}, bf16[4,64,24,128]{3,2,1,0:T(8,128)(2,1)}, ...), condition=%wide.region_4.5_spmd, body=%wide.region_3.4_spmd.sunk | while | flops 403244096 | bytes 18093012 | solution.py:109
  184.6 3.5 %gather_fusion = bf16[24,64,1024]{2,1,0:T(8,128)(2,1)S(1)} fusion(bf16[48,64,1024]{2,1,0:T(8,128)(2,1)} %get-tuple-element.145, s32[1024]{0:T(1024)S(1)} %pad_clamp_fusion.4), kind=kCustom, calls=%fused_computation.clone.1 | custom fusion | bytes 6291552 | tf_op jit(solution)/shard_map/while/body/eval_jaxpr/gather | solution.py:105
  188.2 1.0 constant_dynamic-slice_fusion.3
  189.2 5.1 %fusion.68 = bf16[1,64,24,128]{3,1,2,0:T(8,128)(2,1)S(1)} fusion(bf16[24,64,1024]{2,1,0:T(8,128)(2,1)S(1)} %gather_fusion, bf16[24,128,1024]{2,1,0:T(8,128)(2,1)} %get-tuple-element.146, bf16[1,64,24,128]{3,2,1,0:T(8,128)(2,1)S(1)} %constant_dynamic-slice_fusion.3), kind=kOutput, calls=%fused_computation.8.clone.1 | convolution fusion | flops 403243008 | bytes 10223616 | tf_op jit(solution)/shard_map/while/body/eval_jaxpr/jbp,jqp->bjq/dot_general | solution.py:106
  196.0 3.5 %gather_fusion = bf16[24,64,1024]{2,1,0:T(8,128)(2,1)S(1)} fusion(bf16[48,64,1024]{2,1,0:T(8,128)(2,1)} %get-tuple-element.145, s32[1024]{0:T(1024)S(1)} %pad_clamp_fusion.4), kind=kCustom, calls=%fused_computation.clone.1 | custom fusion | bytes 6291552 | tf_op jit(solution)/shard_map/while/body/eval_jaxpr/gather | solution.py:105
  199.5 1.0 constant_dynamic-slice_fusion.3
  200.6 5.1 %fusion.68 = bf16[1,64,24,128]{3,1,2,0:T(8,128)(2,1)S(1)} fusion(bf16[24,64,1024]{2,1,0:T(8,128)(2,1)S(1)} %gather_fusion, bf16[24,128,1024]{2,1,0:T(8,128)(2,1)} %get-tuple-element.146, bf16[1,64,24,128]{3,2,1,0:T(8,128)(2,1)S(1)} %constant_dynamic-slice_fusion.3), kind=kOutput, calls=%fused_computation.8.clone.1 | convolution fusion | flops 403243008 | bytes 10223616 | tf_op jit(solution)/shard_map/while/body/eval_jaxpr/jbp,jqp->bjq/dot_general | solution.py:106
  207.3 3.5 %gather_fusion = bf16[24,64,1024]{2,1,0:T(8,128)(2,1)S(1)} fusion(bf16[48,64,1024]{2,1,0:T(8,128)(2,1)} %get-tuple-element.145, s32[1024]{0:T(1024)S(1)} %pad_clamp_fusion.4), kind=kCustom, calls=%fused_computation.clone.1 | custom fusion | bytes 6291552 | tf_op jit(solution)/shard_map/while/body/eval_jaxpr/gather | solution.py:105
  210.9 1.0 constant_dynamic-slice_fusion.3
  211.9 5.1 %fusion.68 = bf16[1,64,24,128]{3,1,2,0:T(8,128)(2,1)S(1)} fusion(bf16[24,64,1024]{2,1,0:T(8,128)(2,1)S(1)} %gather_fusion, bf16[24,128,1024]{2,1,0:T(8,128)(2,1)} %get-tuple-element.146, bf16[1,64,24,128]{3,2,1,0:T(8,128)(2,1)S(1)} %constant_dynamic-slice_fusion.3), kind=kOutput, calls=%fused_computation.8.clone.1 | convolution fusion | flops 403243008 | bytes 10223616 | tf_op jit(solution)/shard_map/while/body/eval_jaxpr/jbp,jqp->bjq/dot_general | solution.py:106
  218.7 3.5 %gather_fusion = bf16[24,64,1024]{2,1,0:T(8,128)(2,1)S(1)} fusion(bf16[48,64,1024]{2,1,0:T(8,128)(2,1)} %get-tuple-element.145, s32[1024]{0:T(1024)S(1)} %pad_clamp_fusion.4), kind=kCustom, calls=%fused_computation.clone.1 | custom fusion | bytes 6291552 | tf_op jit(solution)/shard_map/while/body/eval_jaxpr/gather | solution.py:105
  222.2 1.0 constant_dynamic-slice_fusion.3
  223.3 5.1 %fusion.68 = bf16[1,64,24,128]{3,1,2,0:T(8,128)(2,1)S(1)} fusion(bf16[24,64,1024]{2,1,0:T(8,128)(2,1)S(1)} %gather_fusion, bf16[24,128,1024]{2,1,0:T(8,128)(2,1)} %get-tuple-element.146, bf16[1,64,24,128]{3,2,1,0:T(8,128)(2,1)S(1)} %constant_dynamic-slice_fusion.3), kind=kOutput, calls=%fused_computation.8.clone.1 | convolution fusion | flops 403243008 | bytes 10223616 | tf_op jit(solution)/shard_map/while/body/eval_jaxpr/jbp,jqp->bjq/dot_general | solution.py:106
  229.4 3.0 %copy.25 = bf16[32,8,24,128]{3,1,2,0:T(8,128)(2,1)} copy(bf16[32,8,24,128]{3,2,1,0:T(8,128)(2,1)} %bitcast.33) | data formatting | bytes 3145728
  (58 shorter events, 12.5 us)
Async XLA Ops:
  6.5 1.5 copy-start
  8.0 35.3 %copy-start.3 = (bf16[512,1024]{1,0:T(8,128)(2,1)S(1)}, bf16[512,1024]{1,0:T(8,128)(2,1)}, u32[]{:S(2)}) copy-start(bf16[512,1024]{1,0:T(8,128)(2,1)} %param.13) | copy-start | bytes 3145732
  9.6 32.1 %all-to-all-start.1 = ((bf16[8,64,1024]{2,1,0:T(8,128)(2,1)}), bf16[8,64,1024]{2,1,0:T(8,128)(2,1)S(1)}, u32[]{:S(2)}, u32[]{:S(2)}) async-start(bf16[8,64,1024]{2,1,0:T(8,128)(2,1)} %gather_fusion.3), calls=%async_computation.1 | async-start | bytes 2097152 | tf_op jit(solution)/shard_map/all_to_all | solution.py:89
  16.0 70.5 %all-gather.5.cloned.1.call-start = ((), (), s32[]{:S(2)}) async-start(), calls=%async_computation.3 | async-start | bytes 3932160 | tf_op jit(solution)/shard_map/all_gather | solution.py:97
  43.3 110.1 %all-gather.3.cloned.1.call-start = ((), (), s32[]{:S(2)}) async-start(), calls=%async_computation.2 | async-start | bytes 7077888 | tf_op jit(solution)/shard_map/all_gather | solution.py:95
  72.8 4.6 %copy-start.4 = (bf16[2,256,256]{2,1,0:T(8,128)(2,1)S(1)}, bf16[2,256,256]{2,1,0:T(8,128)(2,1)}, u32[]{:S(2)}) copy-start(bf16[2,256,256]{2,1,0:T(8,128)(2,1)} %param.16) | copy-start | bytes 786436
  72.8 4.6 %copy-start.7 = (bf16[2,256,256]{2,1,0:T(8,128)(2,1)S(1)}, bf16[2,256,256]{2,1,0:T(8,128)(2,1)}, u32[]{:S(2)}) copy-start(bf16[2,256,256]{2,1,0:T(8,128)(2,1)} %param.19) | copy-start | bytes 786436
  74.5 3.4 %copy-start.5 = (bf16[2,256,256]{2,1,0:T(8,128)(2,1)S(1)}, bf16[2,256,256]{2,1,0:T(8,128)(2,1)}, u32[]{:S(2)}) copy-start(bf16[2,256,256]{2,1,0:T(8,128)(2,1)} %param.17) | copy-start | bytes 786436
  74.5 3.4 %copy-start.6 = (bf16[2,256,256]{2,1,0:T(8,128)(2,1)S(1)}, bf16[2,256,256]{2,1,0:T(8,128)(2,1)}, u32[]{:S(2)}) copy-start(bf16[2,256,256]{2,1,0:T(8,128)(2,1)} %param.18) | copy-start | bytes 786436
  160.2 1.7 copy-start.2
  229.4 3.0 %copy-start.1 = (bf16[512,1024]{1,0:T(8,128)(2,1)S(1)}, bf16[512,1024]{1,0:T(8,128)(2,1)}, u32[]{:S(2)}) copy-start(bf16[512,1024]{1,0:T(8,128)(2,1)} %param.14) | copy-start | bytes 3145732
Sparse Core Ops, SparseCore 0:
  43.4 43.0 all-gather.4
  88.1 65.1 all-gather.2
where the time goes:
time: 240 us; the launch traced here: 239 us
  waiting for transfers between devices  93.1 us (39%)
  local copies, waits for them, and re-layouts  54.9 us (23%)
  matrix products  31.6 us (13%)
  blocking collectives  28.9 us (12%)
  between operations  13.6 us (6%)
  other arithmetic  10.6 us (4%)
  starting transfers between devices  6.42 us (3%)
    all_gather x1, waiting for transfers between devices, local(): lax.all_gather(own_x, 'col', axis=0, tiled=True)  59.5 us
    all_to_all x1, blocking collectives, local(): lax.all_to_all(held_x[send_slots], 'col', split_axis=0, concat_axis=0, ti...  28.9 us
    all_to_all x1, waiting for transfers between devices, local(): lax.all_to_all(held_y[send_slots], 'col', split_axis=0, concat_axis=0, ti...  25.7 us
    dot_general x4, matrix products, one_slot(): jnp.einsum('jbp,jqp->bjq', picked, stacked, preferred_element_type=jnp.fl...  20.2 us
    gather x4, local copies, waits for them, and re-layouts, one_slot(): picked = lower_blocks[pattern_rows]  14.1 us
    concatenate x1, local copies, waits for them, and re-layouts, join_panels(): jnp.concatenate([left_part[:, :PANEL], right_part[:, :PANEL], left_part[:...  8.62 us
    dot_general x1, matrix products, form_rows(): jnp.dot(remainder, real_form(inv_second), preferred_element_type=jnp.floa...  8.12 us
    all_gather x1, waiting for transfers between devices, local(): lax.all_gather(own_y, 'row', axis=0, tiled=True)  7.82 us
  transfers between devices with their start and end apart: 3, of which 3 were waited for; matrix products, arithmetic and copies ran while one was open for 6% of the time, Pallas kernels for 0%

commit v1 on v0

v1 whole, which is shorter than its diff:
```python
import functools

import jax
import jax.numpy as jnp
from jax import lax
from jax.experimental import pallas as pl
from jax.experimental.pallas import tpu as pltpu
from jax.sharding import PartitionSpec as P

BS = 64
PANEL = 256
PER = 6
PARTS = 4
CH = 2 * PANEL // PARTS
MESH = pl.DeviceIdType.MESH
F32 = jnp.float32
BF16 = jnp.bfloat16


def dot_t(a, b):
    return lax.dot_general(a, b, (((1,), (1,)), ((), ())), preferred_element_type=F32)


def half(block, at):
    lo = at * PANEL
    return jnp.concatenate(
        [block[:, lo : lo + PANEL], block[:, 2 * PANEL + lo : 3 * PANEL + lo]], axis=1
    )


def stacked(w_real, w_imag):
    return jnp.concatenate(
        [
            jnp.concatenate([w_real, -w_imag], axis=1),
            jnp.concatenate([w_imag, w_real], axis=1),
        ],
        axis=0,
    )


def w_part(w_half, p):
    at = (p % 2) * CH
    return stacked(w_half[:, at : at + CH], w_half[:, PANEL + at : PANEL + at + CH])


def body(sizes, *refs):
    rows, cols, cap, fill, width, fused = sizes
    slots_ref, lidx_ref, widx_ref, x_ref, y_ref, inv1, inv2, cr, cl = refs[:9]
    refs = refs[9:]
    if fused:
        trail_ref, out_ref = refs[:2]
        refs = refs[2:]
    l_all, w_all = refs[:PARTS], refs[PARTS : PARTS + 2]
    refs = refs[PARTS + 2 :]
    if fused:
        acc, trail_v, trail_sem = refs[:3]
        refs = refs[3:]
    own_l, stage, w_low, rf, gt, ysend, yrecv, wsend, wrecv, lsend, lrecv, lcopy, ycopy = refs
    row = lax.axis_index("row")
    col = lax.axis_index("col")
    chips = cols // 2
    z = col // 2
    core = col % 2
    tile = 4
    n_tiles = cap // tile

    if fused:
        trail_copy = pltpu.make_async_copy(trail_ref, trail_v, trail_sem)
        trail_copy.start()

    barrier = pltpu.get_barrier_semaphore()
    for d in range(1, cols):
        pl.semaphore_signal(
            barrier, inc=1, device_id=(row, lax.rem(col + d, cols)), device_id_type=MESH
        )
    for d in range(1, rows):
        pl.semaphore_signal(
            barrier, inc=1, device_id=(lax.rem(row + d, rows), col), device_id_type=MESH
        )

    for c in range(cols):
        stage[0, c] = half(y_ref[slots_ref[c]], 0)

    pl.semaphore_wait(barrier, cols + rows - 2)

    def send_y(h):
        for d in range(1, cols):
            to = lax.rem(col + d, cols)
            pltpu.make_async_remote_copy(
                src_ref=stage.at[h, to],
                dst_ref=w_all[h].at[row * cols + col],
                send_sem=ysend.at[h, to],
                recv_sem=yrecv.at[h, col],
                device_id=(row, to),
                device_id_type=MESH,
            ).start()
        pltpu.make_async_copy(
            stage.at[h, col], w_all[h].at[row * cols + col], ycopy.at[h]
        ).start()

    def y_copy(h, o):
        return pltpu.make_async_remote_copy(
            src_ref=stage.at[h, o],
            dst_ref=w_all[h].at[row * cols + o],
            send_sem=ysend.at[h, o],
            recv_sem=yrecv.at[h, o],
            device_id=(row, o),
            device_id_type=MESH,
        )

    def w_copy(h, r, to):
        return pltpu.make_async_remote_copy(
            src_ref=w_all[h].at[pl.ds(r * cols, cols)],
            dst_ref=w_all[h].at[pl.ds(r * cols, cols)],
            send_sem=wsend.at[h, to],
            recv_sem=wrecv.at[h, r],
            device_id=(to, col),
            device_id_type=MESH,
        )

    def spread_w(h):
        for d in range(1, cols):
            y_copy(h, lax.rem(col + d, cols)).wait_recv()
        pltpu.make_async_copy(
            stage.at[h, col], w_all[h].at[row * cols + col], ycopy.at[h]
        ).wait()
        for d in range(1, rows):
            w_copy(h, row, lax.rem(row + d, rows)).start()

    def await_w(h):
        for d in range(1, rows):
            r = lax.rem(row + d, rows)
            w_copy(h, r, r).wait_recv()

    def l_copy(p, o, way, own):
        place = l_all[p].at[pl.ds(o * cap, cap)]
        to = (col - 2, col + 2, col + 1 - 2 * core)[way]
        return pltpu.make_async_remote_copy(
            src_ref=own_l.at[p] if own else place,
            dst_ref=place,
            send_sem=lsend.at[p, o, way],
            recv_sem=lrecv.at[p, o],
            device_id=(row, to),
            device_id_type=MESH,
        )

    def l_own(p):
        return pltpu.make_async_copy(
            own_l.at[p], l_all[p].at[pl.ds(col * cap, cap)], lcopy.at[p]
        )

    def send_own(p):
        @pl.when(z > 0)
        def _():
            l_copy(p, col, 0, True).start()

        @pl.when(z < chips - 1)
        def _():
            l_copy(p, col, 1, True).start()

        l_copy(p, col, 2, True).start()
        l_own(p).start()

    def relay(p):
        for d in range(1, chips):
            left = col - 2 * d
            right = col + 2 * d

            @pl.when(z >= d)
            def _():
                l_copy(p, left, 1, False).wait_recv()

                @pl.when(z < chips - 1)
                def _():
                    l_copy(p, left, 1, False).start()

                l_copy(p, left, 2, False).start()

            @pl.when(z + d < chips)
            def _():
                l_copy(p, right, 0, False).wait_recv()

                @pl.when(z > 0)
                def _():
                    l_copy(p, right, 0, False).start()

                l_copy(p, right, 2, False).start()

    def await_l(p):
        l_own(p).wait()
        for chip in range(chips):
            l_copy(p, 2 * chip + 1 - core, 2, False).wait_recv()

    def l_drain(p):
        @pl.when(z > 0)
        def _():
            l_copy(p, col, 0, True).wait_send()

        @pl.when(z < chips - 1)
        def _():
            l_copy(p, col, 1, True).wait_send()

        l_copy(p, col, 2, True).wait_send()
        for d in range(1, chips):
            left = col - 2 * d
            right = col + 2 * d

            @pl.when(z >= d)
            def _():
                @pl.when(z < chips - 1)
                def _():
                    l_copy(p, left, 1, False).wait_send()

                l_copy(p, left, 2, False).wait_send()

            @pl.when(z + d < chips)
            def _():
                @pl.when(z > 0)
                def _():
                    l_copy(p, right, 0, False).wait_send()

                l_copy(p, right, 2, False).wait_send()

    def set_real_form(at, pair):
        rf[at, :PANEL, :PANEL] = pair[0]
        rf[at, :PANEL, PANEL:] = pair[1]
        rf[at, PANEL:, :PANEL] = -pair[1]
        rf[at, PANEL:, PANEL:] = pair[0]

    send_y(0)

    set_real_form(0, inv1)
    coupling = jnp.dot(
        jnp.concatenate([cl[0], cl[1]], axis=1), rf[0], preferred_element_type=F32
    ).astype(BF16)
    gt[:PANEL, :PANEL] = coupling[:, :PANEL]
    gt[:PANEL, PANEL:] = -coupling[:, PANEL:]
    gt[PANEL:, :PANEL] = coupling[:, PANEL:]
    gt[PANEL:, PANEL:] = coupling[:, :PANEL]

    def low_w(i, carry):
        block = y_ref[pl.ds(i * tile, tile)].reshape(tile * BS, 4 * PANEL)
        low = half(block, 1).astype(F32) - dot_t(half(block, 0), gt[...])
        w_low[pl.ds(i * tile, tile)] = low.astype(BF16).reshape(tile, BS, 2 * PANEL)
        return carry

    lax.fori_loop(0, n_tiles, low_w, 0)
    for c in range(cols):
        stage[1, c] = w_low[slots_ref[c]]
    send_y(1)

    def put_l(i, first, value):
        for k in range(2):
            part = jnp.concatenate(
                [
                    value[:, k * CH : (k + 1) * CH],
                    value[:, PANEL + k * CH : PANEL + (k + 1) * CH],
                ],
                axis=1,
            )
            own_l[first + k, pl.ds(i * tile, tile)] = part.reshape(tile, BS, 2 * CH)

    def first_l(i, carry):
        block = x_ref[pl.ds(i * tile, tile)].reshape(tile * BS, 4 * PANEL)
        value = jnp.dot(half(block, 0), rf[0], preferred_element_type=F32).astype(BF16)
        put_l(i, 0, value)
        return carry

    lax.fori_loop(0, n_tiles, first_l, 0)
    send_own(0)

    set_real_form(1, cr)
    set_real_form(2, inv2)

    def second_l(i, carry):
        block = x_ref[pl.ds(i * tile, tile)].reshape(tile * BS, 4 * PANEL)
        parts = [
            own_l[k, pl.ds(i * tile, tile)].reshape(tile * BS, 2 * CH) for k in range(2)
        ]
        low = jnp.concatenate(
            [parts[0][:, :CH], parts[1][:, :CH], parts[0][:, CH:], parts[1][:, CH:]], axis=1
        )
        rest = half(block, 1).astype(F32) - jnp.dot(low, rf[1], preferred_element_type=F32)
        value = jnp.dot(rest.astype(BF16), rf[2], preferred_element_type=F32).astype(BF16)
        put_l(i, 2, value)
        return carry

    lax.fori_loop(0, n_tiles, second_l, 0)

    def update(p):
        h = p // 2

        def column(q, carry):
            rhs = w_part(w_all[h][widx_ref[q]], p)
            lhs = jnp.concatenate(
                [l_all[p][lidx_ref[s * width + q]] for s in range(fill)], axis=0
            )
            change = dot_t(lhs, rhs)
            lanes = pl.ds(pl.multiple_of(q * 2 * BS, 2 * BS), 2 * BS)
            if p == 0:
                acc[q] = trail_v[:, lanes].astype(F32) - change
            elif p < PARTS - 1:
                acc[q] = acc[q] - change
            else:
                out_ref[:, lanes] = (acc[q] - change).astype(BF16)
            return carry

        lax.fori_loop(0, width, column, 0)

    def finish(p):
        await_l(p)
        if p % 2 == 0:
            await_w(p // 2)
        if fused:
            if p == 0:
                trail_copy.wait()
            update(p)

    spread_w(0)
    relay(0)
    spread_w(1)
    for p in range(1, PARTS):
        send_own(p)
        finish(p - 1)
        relay(p)
    finish(PARTS - 1)

    for h in range(2):
        for d in range(1, cols):
            y_copy(h, lax.rem(col + d, cols)).wait_send()
        for d in range(1, rows):
            w_copy(h, row, lax.rem(row + d, rows)).wait_send()
    for p in range(PARTS):
        l_drain(p)


def pick_body(lidx_ref, widx_ref, *refs):
    l_refs, w_refs = refs[:PARTS], refs[PARTS : PARTS + 2]
    trail_ref, out_ref = refs[PARTS + 2 :]
    total = trail_ref[...].astype(F32)
    for p in range(PARTS):
        total = total - dot_t(l_refs[p][0], w_part(w_refs[p // 2][0], p))
    out_ref[...] = total.astype(BF16)


def plan(trail_rows, owner_of, rows, cols, cap):
    my_row = lax.axis_index("row")
    my_col = lax.axis_index("col")
    count = PER * cols
    grid = owner_of.reshape(rows, count)
    owners = lax.dynamic_index_in_dim(grid, my_row, 0, keepdims=False)
    at = jnp.arange(count, dtype=jnp.int32)
    same = (owners[:, None] == owners[None, :]) & (at[None, :] < at[:, None])
    slot = jnp.sum(same.astype(jnp.int32), axis=1, dtype=jnp.int32)
    place = owners * cap + slot
    lidx = jnp.sum(
        jnp.where(trail_rows[:, :, None] == at, place, 0), axis=2, dtype=jnp.int32
    )
    slots = jnp.sum(
        jnp.where(owners == my_col, slot, 0).reshape(cols, PER), axis=1, dtype=jnp.int32
    )
    wanted = lax.dynamic_index_in_dim(
        owner_of.reshape(rows, cols, PER), my_col, 1, keepdims=False
    )
    widx = wanted + cols * jnp.arange(rows, dtype=jnp.int32)[:, None]
    return slots, lidx.reshape(-1), widx.reshape(-1)


def local(mesh, trail, trail_rows, owner_x, owner_y, owner_of, inv1, inv2, cr, cl):
    rows, cols = mesh.shape["row"], mesh.shape["col"]
    cap = owner_x.shape[0] // BS
    fill = trail.shape[0] // BS
    width = trail.shape[1] // (2 * BS)
    l_shape = (cols * cap, BS, 2 * CH)
    w_shape = (rows * cols, BS, 2 * PANEL)
    fused = cols * cap * BS * 4 * PANEL * 2 <= 16 << 20
    slots, lidx, widx = plan(trail_rows, owner_of, rows, cols, cap)
    blocks = (cap, BS, 4 * PANEL)
    operands = [
        slots, lidx, widx, owner_x.reshape(blocks), owner_y.reshape(blocks), inv1, inv2, cr, cl,
    ]
    smem = pl.BlockSpec(memory_space=pltpu.SMEM)
    vmem = pl.BlockSpec(memory_space=pltpu.VMEM)
    anywhere = pl.BlockSpec(memory_space=pl.ANY)
    in_specs = [smem] * 3 + [vmem] * 6
    scratch = [
        pltpu.VMEM((PARTS, cap, BS, 2 * CH), BF16),
        pltpu.VMEM((2, cols, BS, 2 * PANEL), BF16),
        pltpu.VMEM((cap, BS, 2 * PANEL), BF16),
        pltpu.VMEM((3, 2 * PANEL, 2 * PANEL), BF16),
        pltpu.VMEM((2 * PANEL, 2 * PANEL), BF16),
        pltpu.SemaphoreType.DMA((2, cols)),
        pltpu.SemaphoreType.DMA((2, cols)),
        pltpu.SemaphoreType.DMA((2, rows)),
        pltpu.SemaphoreType.DMA((2, rows)),
        pltpu.SemaphoreType.DMA((PARTS, cols, 3)),
        pltpu.SemaphoreType.DMA((PARTS, cols)),
        pltpu.SemaphoreType.DMA((PARTS,)),
        pltpu.SemaphoreType.DMA((2,)),
    ]
    if fused:
        operands.append(trail)
        in_specs.append(anywhere)
        out_shape = jax.ShapeDtypeStruct(trail.shape, BF16)
        out_specs = vmem
        scratch = [pltpu.VMEM(l_shape, BF16)] * PARTS + [pltpu.VMEM(w_shape, BF16)] * 2 + [
            pltpu.VMEM((width, fill * BS, 2 * BS), F32),
            pltpu.VMEM(trail.shape, BF16),
            pltpu.SemaphoreType.DMA,
        ] + scratch
    else:
        out_shape = [jax.ShapeDtypeStruct(l_shape, BF16)] * PARTS
        out_shape += [jax.ShapeDtypeStruct(w_shape, BF16)] * 2
        out_specs = [anywhere] * (PARTS + 2)
    result = pl.pallas_call(
        functools.partial(body, (rows, cols, cap, fill, width, fused)),
        out_shape=out_shape,
        in_specs=in_specs,
        out_specs=out_specs,
        scratch_shapes=scratch,
        compiler_params=pltpu.CompilerParams(
            collective_id=0, has_side_effects=True, vmem_limit_bytes=48 << 20
        ),
    )(*operands)
    if fused:
        return result
    return pl.pallas_call(
        pick_body,
        out_shape=jax.ShapeDtypeStruct(trail.shape, BF16),
        grid_spec=pltpu.PrefetchScalarGridSpec(
            num_scalar_prefetch=2,
            grid=(width, fill),
            in_specs=[
                pl.BlockSpec((1, BS, 2 * CH), lambda q, s, li, wi: (li[s * width + q], 0, 0))
            ]
            * PARTS
            + [pl.BlockSpec((1, BS, 2 * PANEL), lambda q, s, li, wi: (wi[q], 0, 0))] * 2
            + [pl.BlockSpec((BS, 2 * BS), lambda q, s, li, wi: (s, q))],
            out_specs=pl.BlockSpec((BS, 2 * BS), lambda q, s, li, wi: (s, q)),
        ),
    )(lidx, widx, *result, trail)


def solution(mesh):
    both = P(("row", "col"), None)
    placed = (P("row", "col"), P("row", "col"), both, both, P(), P(), P(), P(), P())
    return jax.shard_map(
        functools.partial(local, mesh),
        mesh=mesh,
        in_specs=placed,
        out_specs=P("row", "col"),
        check_vma=False,
    )
```

time: 240 us -> 123 us (0.51)
  Pallas kernels: 0 us -> 112 us
  waiting for transfers between devices: 93.1 us -> 0 us
  local copies, waits for them, and re-layouts: 54.9 us -> 9.47 us
  matrix products: 31.6 us -> 0 us
  blocking collectives: 28.9 us -> 0 us
  between operations: 13.6 us -> 0.04 us
  other arithmetic: 10.6 us -> 1.25 us
  starting transfers between devices: 6.42 us -> 0 us
    pallas_call x0 -> x1, Pallas kernels: none -> 112 us  [local(): pl.pallas_call(functools.partial(body, (rows, cols, cap, fill, width, fus...]
    all_gather x2 -> x0, waiting for transfers between devices: 67.3 us -> none  [the longest x1 59.5 us: local(): lax.all_gather(own_x, 'col', axis=0, tiled=True)]
    dot_general x8 -> x0, matrix products: 31.6 us -> none  [the longest x4 20.2 us: one_slot(): jnp.einsum('jbp,jqp->bjq', picked, stacked, preferred_element_type=jnp.fl...]
    all_to_all x1 -> x0, blocking collectives: 28.9 us -> none  [local(): lax.all_to_all(held_x[send_slots], 'col', split_axis=0, concat_axis=0, ti...]
    all_to_all x1 -> x0, waiting for transfers between devices: 25.7 us -> none  [local(): lax.all_to_all(held_y[send_slots], 'col', split_axis=0, concat_axis=0, ti...]
    gather x8 -> x0, local copies, waits for them, and re-layouts: 19.4 us -> none  [the longest x4 14.1 us: one_slot(): picked = lower_blocks[pattern_rows]]
    slice x5 -> x0, local copies, waits for them, and re-layouts: 9.41 us -> none  [the longest x1 4.93 us: halves(): matrix[:, PANEL:2 * PANEL]]
    concatenate x1 -> x0, local copies, waits for them, and re-layouts: 8.62 us -> none  [join_panels(): jnp.concatenate([left_part[:, :PANEL], right_part[:, :PANEL], left_part[:...]
  transfers between devices with their start and end apart: 3 -> 0, of which waited for: 3 -> 0; matrix products, arithmetic and copies ran while one was open for 6% -> 0% of each run, Pallas kernels for 0% -> 0%
where the time goes in v1:
time: 123 us; the launch traced here: 122 us
  Pallas kernels  112 us (91%)
  local copies, waits for them, and re-layouts  9.47 us (8%)
  other arithmetic  1.25 us (1%)
    pallas_call x1, Pallas kernels, local(): pl.pallas_call(functools.partial(body, (rows, cols, cap, fill, width, fus...  112 us
    unnamed x13, local copies, waits for them, and re-layouts  7.4 us

profile of v1, /device:TPU:1, one launch (start us, length us, event | category | flops | bytes accessed | tf_op | source)
XLA Modules:
  0.0 122.4 jit_solution(8765117585451326609)
XLA Ops:
  0.0 0.1 add.25
  0.1 0.1 add.26
  0.2 0.8 reshape.31
  1.0 0.1 eq.40
  1.0 0.2 convert_reduce_fusion
  1.3 0.9 select_reduce_fusion
  2.1 0.1 reshape.32.refs_1_
  2.2 0.1 reduce_sum.30
  2.3 0.1 select_reduce_fusion.1.refs_0_
  2.4 0.8 reshape.33
  3.3 0.1 squeeze.6
  3.3 0.0 copy-start
  3.3 1.2 %copy-done = bf16[512,1024]{1,0:T(8,128)(2,1)S(1)} copy-done((bf16[512,1024]{1,0:T(8,128)(2,1)S(1)}, bf16[512,1024]{1,0:T(8,128)(2,1)}, u32[]{:S(2)}) %copy-start) | copy-done | bytes 1048600
  4.6 0.0 copy-start.1
  4.6 1.2 copy-done.1
  5.8 0.0 copy-start.2
  5.8 0.9 copy-done.2
  6.8 0.0 copy-start.3
  6.8 0.9 copy-done.3
  7.7 0.0 copy-start.4
  7.7 0.9 copy-done.4
  8.7 0.0 copy-start.5
  8.7 0.9 copy-done.5
  9.6 111.6 %shard_map.91 = bf16[256,3072]{1,0:T(8,128)(2,1)S(1)} custom-call(s32[8]{0:T(128)S(1)} %select_reduce_fusion.1.refs_0_, s32[96]{0:T(128)S(1)} %reshape.32.refs_1_, s32[24]{0:T(128)S(1)} %add.27.refs_2_, bf16[8,64,1024]{2,1,0:T(8,128)(2,1)S(1)} %bitcast.6, bf16[8,64,1024]{2,1,0:T(8,128)(2,1)S(1)} %bitcast.7, bf16[2,256,256]{2,1,0:T(8,128)(2,1)S(1)} %copy-done.2, ...), custom_call_target="tpu_custom_call" | custom-call | tf_op jit(solution)/shard_map/pallas_call | solution.py:415
  121.2 1.1 copy.11
  (6 shorter events, 0.1 us)
Async XLA Ops:
  3.3 1.2 %copy-start = (bf16[512,1024]{1,0:T(8,128)(2,1)S(1)}, bf16[512,1024]{1,0:T(8,128)(2,1)}, u32[]{:S(2)}) copy-start(bf16[512,1024]{1,0:T(8,128)(2,1)} %param.11) | copy-start | bytes 3145732
  4.6 1.2 %copy-start.1 = (bf16[512,1024]{1,0:T(8,128)(2,1)S(1)}, bf16[512,1024]{1,0:T(8,128)(2,1)}, u32[]{:S(2)}) copy-start(bf16[512,1024]{1,0:T(8,128)(2,1)} %param.12) | copy-start | bytes 3145732
  5.8 0.9 copy-start.2
  6.8 0.9 copy-start.3
  7.7 0.9 copy-start.4
  8.7 0.9 copy-start.5

commit v2 on v1

--- a/solution.py
+++ b/solution.py
@@ -45,7 +45,8 @@
 
 def body(sizes, *refs):
     rows, cols, cap, fill, width, fused = sizes
-    slots_ref, lidx_ref, widx_ref, x_ref, y_ref, inv1, inv2, cr, cl = refs[:9]
+    place_ref, owner_ref, picks_ref = refs[:3]
+    sources = refs[3:9]
     refs = refs[9:]
     if fused:
         trail_ref, out_ref = refs[:2]
@@ -55,7 +56,10 @@
     if fused:
         acc, trail_v, trail_sem = refs[:3]
         refs = refs[3:]
-    own_l, stage, w_low, rf, gt, ysend, yrecv, wsend, wrecv, lsend, lrecv, lcopy, ycopy = refs
+    own_l, stage, w_low, rf, gt = refs[:5]
+    held = refs[5:11]
+    y_ref, cl, inv1, x_ref, cr, inv2 = held
+    fetched, ysend, yrecv, wsend, wrecv, lsend, lrecv, lcopy, ycopy = refs[11:]
     row = lax.axis_index("row")
     col = lax.axis_index("col")
     chips = cols // 2
@@ -64,6 +68,11 @@
     tile = 4
     n_tiles = cap // tile
 
+    fetch = [
+        pltpu.make_async_copy(sources[i], held[i], fetched.at[i]) for i in range(len(held))
+    ]
+    for copy in fetch:
+        copy.start()
     if fused:
         trail_copy = pltpu.make_async_copy(trail_ref, trail_v, trail_sem)
         trail_copy.start()
@@ -78,8 +87,17 @@
             barrier, inc=1, device_id=(lax.rem(row + d, rows), col), device_id_type=MESH
         )
 
+    slots = []
     for c in range(cols):
-        stage[0, c] = half(y_ref[slots_ref[c]], 0)
+        slot = 0
+        for k in range(c * PER, (c + 1) * PER):
+            mine = owner_ref[row * (PER * cols) + k] == col
+            slot = slot + jnp.where(mine, place_ref[k] - col * cap, 0)
+        slots.append(slot)
+
+    fetch[0].wait()
+    for c in range(cols):
+        stage[0, c] = half(y_ref[slots[c]], 0)
 
     pl.semaphore_wait(barrier, cols + rows - 2)
 
@@ -149,6 +167,9 @@
             own_l.at[p], l_all[p].at[pl.ds(col * cap, cap)], lcopy.at[p]
         )
 
+    leftmost = z < chips // 2
+    at_end = (z == 0) | (z == chips - 1)
+
     def send_own(p):
         @pl.when(z > 0)
         def _():
@@ -161,30 +182,44 @@
         l_copy(p, col, 2, True).start()
         l_own(p).start()
 
+    def relay_left(p, d):
+        left = col - 2 * d
+
+        @pl.when(z >= d)
+        def _():
+            l_copy(p, left, 1, False).wait_recv()
+
+            @pl.when(z < chips - 1)
+            def _():
+                l_copy(p, left, 1, False).start()
+
+            l_copy(p, left, 2, False).start()
+
+    def relay_right(p, d):
+        right = col + 2 * d
+
+        @pl.when(z + d < chips)
+        def _():
+            l_copy(p, right, 0, False).wait_recv()
+
+            @pl.when(z > 0)
+            def _():
+                l_copy(p, right, 0, False).start()
+
+            l_copy(p, right, 2, False).start()
+
     def relay(p):
-        for d in range(1, chips):
-            left = col - 2 * d
-            right = col + 2 * d
-
-            @pl.when(z >= d)
-            def _():
-                l_copy(p, left, 1, False).wait_recv()
-
-                @pl.when(z < chips - 1)
-                def _():
-                    l_copy(p, left, 1, False).start()
-
-                l_copy(p, left, 2, False).start()
-
-            @pl.when(z + d < chips)
-            def _():
-                l_copy(p, right, 0, False).wait_recv()
-
-                @pl.when(z > 0)
-                def _():
-                    l_copy(p, right, 0, False).start()
-
-                l_copy(p, right, 2, False).start()
+        @pl.when(leftmost)
+        def _():
+            for d in range(1, chips):
+                relay_right(p, d)
+                relay_left(p, d)
+
+        @pl.when(jnp.logical_not(leftmost))
+        def _():
+            for d in range(1, chips):
+                relay_left(p, d)
+                relay_right(p, d)
 
     def await_l(p):
         l_own(p).wait()
@@ -229,6 +264,8 @@
 
     send_y(0)
 
+    fetch[1].wait()
+    fetch[2].wait()
     set_real_form(0, inv1)
     coupling = jnp.dot(
         jnp.concatenate([cl[0], cl[1]], axis=1), rf[0], preferred_element_type=F32
@@ -246,7 +283,7 @@
 
     lax.fori_loop(0, n_tiles, low_w, 0)
     for c in range(cols):
-        stage[1, c] = w_low[slots_ref[c]]
+        stage[1, c] = w_low[slots[c]]
     send_y(1)
 
     def put_l(i, first, value):
@@ -266,8 +303,11 @@
         put_l(i, 0, value)
         return carry
 
+    fetch[3].wait()
     lax.fori_loop(0, n_tiles, first_l, 0)
     send_own(0)
+    fetch[4].wait()
+    fetch[5].wait()
 
     set_real_form(1, cr)
     set_real_form(2, inv2)
@@ -291,9 +331,11 @@
         h = p // 2
 
         def column(q, carry):
-            rhs = w_part(w_all[h][widx_ref[q]], p)
+            group = q // PER
+            owner = owner_ref[(group * cols + col) * PER + q % PER]
+            rhs = w_part(w_all[h][group * cols + owner], p)
             lhs = jnp.concatenate(
-                [l_all[p][lidx_ref[s * width + q]] for s in range(fill)], axis=0
+                [l_all[p][place_ref[picks_ref[s, q]]] for s in range(fill)], axis=0
             )
             change = dot_t(lhs, rhs)
             lanes = pl.ds(pl.multiple_of(q * 2 * BS, 2 * BS), 2 * BS)
@@ -316,13 +358,32 @@
                 trail_copy.wait()
             update(p)
 
+    @pl.when(at_end)
+    def _():
+        for p in range(1, PARTS):
+            send_own(p)
+
     spread_w(0)
     relay(0)
     spread_w(1)
     for p in range(1, PARTS):
-        send_own(p)
-        finish(p - 1)
+
+        @pl.when(jnp.logical_not(at_end))
+        def _():
+            send_own(p)
+            if p > 1:
+                finish(p - 2)
+
+        @pl.when(at_end)
+        def _():
+            finish(p - 1)
+
         relay(p)
+
+    @pl.when(jnp.logical_not(at_end))
+    def _():
+        finish(PARTS - 2)
+
     finish(PARTS - 1)
 
     for h in range(2):
@@ -343,27 +404,24 @@
     out_ref[...] = total.astype(BF16)
 
 
-def plan(trail_rows, owner_of, rows, cols, cap):
-    my_row = lax.axis_index("row")
-    my_col = lax.axis_index("col")
+def plan(owner_of, rows, cols, cap):
     count = PER * cols
-    grid = owner_of.reshape(rows, count)
-    owners = lax.dynamic_index_in_dim(grid, my_row, 0, keepdims=False)
+    owners = lax.dynamic_slice_in_dim(owner_of, lax.axis_index("row") * count, count)
     at = jnp.arange(count, dtype=jnp.int32)
     same = (owners[:, None] == owners[None, :]) & (at[None, :] < at[:, None])
-    slot = jnp.sum(same.astype(jnp.int32), axis=1, dtype=jnp.int32)
-    place = owners * cap + slot
+    return owners * cap + jnp.sum(same.astype(jnp.int32), axis=1, dtype=jnp.int32)
+
+
+def pick_indices(place, trail_rows, owner_of, rows, cols):
+    at = jnp.arange(place.shape[0], dtype=jnp.int32)
     lidx = jnp.sum(
         jnp.where(trail_rows[:, :, None] == at, place, 0), axis=2, dtype=jnp.int32
     )
-    slots = jnp.sum(
-        jnp.where(owners == my_col, slot, 0).reshape(cols, PER), axis=1, dtype=jnp.int32
-    )
     wanted = lax.dynamic_index_in_dim(
-        owner_of.reshape(rows, cols, PER), my_col, 1, keepdims=False
+        owner_of.reshape(rows, cols, PER), lax.axis_index("col"), 1, keepdims=False
     )
     widx = wanted + cols * jnp.arange(rows, dtype=jnp.int32)[:, None]
-    return slots, lidx.reshape(-1), widx.reshape(-1)
+    return lidx.reshape(-1), widx.reshape(-1)
 
 
 def local(mesh, trail, trail_rows, owner_x, owner_y, owner_of, inv1, inv2, cr, cl):
@@ -374,21 +432,23 @@
     l_shape = (cols * cap, BS, 2 * CH)
     w_shape = (rows * cols, BS, 2 * PANEL)
     fused = cols * cap * BS * 4 * PANEL * 2 <= 16 << 20
-    slots, lidx, widx = plan(trail_rows, owner_of, rows, cols, cap)
+    place = plan(owner_of, rows, cols, cap)
     blocks = (cap, BS, 4 * PANEL)
-    operands = [
-        slots, lidx, widx, owner_x.reshape(blocks), owner_y.reshape(blocks), inv1, inv2, cr, cl,
-    ]
+    fetched = [owner_y.reshape(blocks), cl, inv1, owner_x.reshape(blocks), cr, inv2]
+    operands = [place, owner_of, trail_rows] + fetched
     smem = pl.BlockSpec(memory_space=pltpu.SMEM)
     vmem = pl.BlockSpec(memory_space=pltpu.VMEM)
     anywhere = pl.BlockSpec(memory_space=pl.ANY)
-    in_specs = [smem] * 3 + [vmem] * 6
+    hbm = pl.BlockSpec(memory_space=pltpu.HBM)
+    in_specs = [smem] * 3 + [hbm] * len(fetched)
     scratch = [
         pltpu.VMEM((PARTS, cap, BS, 2 * CH), BF16),
         pltpu.VMEM((2, cols, BS, 2 * PANEL), BF16),
         pltpu.VMEM((cap, BS, 2 * PANEL), BF16),
         pltpu.VMEM((3, 2 * PANEL, 2 * PANEL), BF16),
         pltpu.VMEM((2 * PANEL, 2 * PANEL), BF16),
+        *[pltpu.VMEM(array.shape, BF16) for array in fetched],
+        pltpu.SemaphoreType.DMA((len(fetched),)),
         pltpu.SemaphoreType.DMA((2, cols)),
         pltpu.SemaphoreType.DMA((2, cols)),
         pltpu.SemaphoreType.DMA((2, rows)),
@@ -400,7 +460,7 @@
     ]
     if fused:
         operands.append(trail)
-        in_specs.append(anywhere)
+        in_specs.append(hbm)
         out_shape = jax.ShapeDtypeStruct(trail.shape, BF16)
         out_specs = vmem
         scratch = [pltpu.VMEM(l_shape, BF16)] * PARTS + [pltpu.VMEM(w_shape, BF16)] * 2 + [
@@ -419,11 +479,12 @@
         out_specs=out_specs,
         scratch_shapes=scratch,
         compiler_params=pltpu.CompilerParams(
-            collective_id=0, has_side_effects=True, vmem_limit_bytes=48 << 20
+            collective_id=0, has_side_effects=True, vmem_limit_bytes=60 << 20
         ),
     )(*operands)
     if fused:
         return result
+    lidx, widx = pick_indices(place, trail_rows, owner_of, rows, cols)
     return pl.pallas_call(
         pick_body,
         out_shape=jax.ShapeDtypeStruct(trail.shape, BF16),

time: 123 us -> 114 us (0.927)
  local copies, waits for them, and re-layouts: 9.47 us -> 3.4 us
  Pallas kernels: 112 us -> 109 us
    unnamed x13 -> x1, local copies, waits for them, and re-layouts: 7.4 us -> 2.65 us
    pallas_call x1, Pallas kernels: 112 us -> 109 us  [local(): pl.pallas_call(functools.partial(body, (rows, cols, cap, fill, width, fus...]
    reshape x3 -> x0, local copies, waits for them, and re-layouts: 1.63 us -> none  [the longest x1 0.78 us: plan(): owner_of.reshape(rows, cols, PER)]
    add x2 -> x1, other arithmetic: 0.02 us -> 1.27 us  [plan(): owners * cap + jnp.sum(same.astype(jnp.int32), axis=1, dtype=jnp.int32)]
where the time goes in v2:
time: 114 us
  Pallas kernels  109 us (96%)
  local copies, waits for them, and re-layouts  3.4 us (3%)
  other arithmetic  1.45 us (1%)
    pallas_call x1, Pallas kernels, local(): pl.pallas_call(functools.partial(body, (rows, cols, cap, fill, width, fus...  109 us
    unnamed x1, local copies, waits for them, and re-layouts  2.65 us

profile of v2, /device:TPU:1, one launch (start us, length us, event | category | flops | bytes accessed | tf_op | source)
XLA Modules:
  0.0 113.6 jit_solution(8277778998231586157)
XLA Ops:
  0.0 0.8 dynamic_slice.3
  0.8 0.2 convert_reduce_fusion
  0.9 1.3 %multiply_add_fusion.refs_0_ = s32[48]{0:T(128)} fusion(s32[48]{0:T(128)S(1)} %convert_reduce_fusion, s32[192]{0:T(256)} %refs_1_.1, s32[]{:T(128)S(6)} %select_n.3), kind=kLoop, calls=%fused_computation.3 | loop fusion | flops 96 | bytes 580 | tf_op jit(solution)/shard_map/add | solution.py:412
  2.2 108.7 %shard_map.91 = bf16[256,3072]{1,0:T(8,128)(2,1)} custom-call(s32[48]{0:T(128)} %multiply_add_fusion.refs_0_, s32[192]{0:T(256)} %refs_1_.1, s32[4,24]{1,0:T(4,128)} %refs_2_.1, bf16[8,64,1024]{2,1,0:T(8,128)(2,1)} %bitcast.2, bf16[2,256,256]{2,1,0:T(8,128)(2,1)} %refs_4_.1, bf16[2,256,256]{2,1,0:T(8,128)(2,1)} %refs_5_.1, bf16[8,64,1024]{2,1,0:T(8,128)(2,1)} %bitcast.3, ...), custom_call_target="tpu_custom_call" | custom-call | tf_op jit(solution)/shard_map/pallas_call | solution.py:475
  110.9 2.7 %copy.11 = bf16[256,3072]{1,0:T(8,128)(2,1)} copy(bf16[256,3072]{1,0:T(8,128)(2,1)} %shard_map.91) | data formatting | bytes 3145728

commit v3 on v2

--- a/solution.py
+++ b/solution.py
@@ -45,9 +45,9 @@
 
 def body(sizes, *refs):
     rows, cols, cap, fill, width, fused = sizes
-    place_ref, owner_ref, picks_ref = refs[:3]
-    sources = refs[3:9]
-    refs = refs[9:]
+    owner_ref, picks_ref = refs[:2]
+    sources = refs[2:8]
+    refs = refs[8:]
     if fused:
         trail_ref, out_ref = refs[:2]
         refs = refs[2:]
@@ -59,7 +59,7 @@
     own_l, stage, w_low, rf, gt = refs[:5]
     held = refs[5:11]
     y_ref, cl, inv1, x_ref, cr, inv2 = held
-    fetched, ysend, yrecv, wsend, wrecv, lsend, lrecv, lcopy, ycopy = refs[11:]
+    place_ref, fetched, ysend, yrecv, wsend, wrecv, lsend, lrecv, lcopy, ycopy = refs[11:]
     row = lax.axis_index("row")
     col = lax.axis_index("col")
     chips = cols // 2
@@ -88,12 +88,14 @@
         )
 
     slots = []
+    met = jnp.int32(0)
     for c in range(cols):
-        slot = 0
+        slot = jnp.int32(0)
         for k in range(c * PER, (c + 1) * PER):
             mine = owner_ref[row * (PER * cols) + k] == col
-            slot = slot + jnp.where(mine, place_ref[k] - col * cap, 0)
-        slots.append(slot)
+            slot = jnp.where(mine, met, slot)
+            met = met + jnp.where(mine, 1, 0)
+        slots.append(jnp.minimum(slot, cap - 1))
 
     fetch[0].wait()
     for c in range(cols):
@@ -347,7 +349,7 @@
                 out_ref[:, lanes] = (acc[q] - change).astype(BF16)
             return carry
 
-        lax.fori_loop(0, width, column, 0)
+        lax.fori_loop(0, width, column, 0, unroll=4)
 
     def finish(p):
         await_l(p)
@@ -362,6 +364,18 @@
     def _():
         for p in range(1, PARTS):
             send_own(p)
+
+    def rank(b, counts):
+        owner = owner_ref[row * (PER * cols) + b]
+        slot = jnp.int32(0)
+        after = []
+        for c in range(cols):
+            slot = jnp.where(owner == c, counts[c], slot)
+            after.append(counts[c] + jnp.where(owner == c, 1, 0))
+        place_ref[b] = owner * cap + jnp.minimum(slot, cap - 1)
+        return tuple(after)
+
+    lax.fori_loop(0, PER * cols, rank, (jnp.int32(0),) * cols)
 
     spread_w(0)
     relay(0)
@@ -432,15 +446,14 @@
     l_shape = (cols * cap, BS, 2 * CH)
     w_shape = (rows * cols, BS, 2 * PANEL)
     fused = cols * cap * BS * 4 * PANEL * 2 <= 16 << 20
-    place = plan(owner_of, rows, cols, cap)
     blocks = (cap, BS, 4 * PANEL)
     fetched = [owner_y.reshape(blocks), cl, inv1, owner_x.reshape(blocks), cr, inv2]
-    operands = [place, owner_of, trail_rows] + fetched
+    operands = [owner_of, trail_rows] + fetched
     smem = pl.BlockSpec(memory_space=pltpu.SMEM)
     vmem = pl.BlockSpec(memory_space=pltpu.VMEM)
     anywhere = pl.BlockSpec(memory_space=pl.ANY)
     hbm = pl.BlockSpec(memory_space=pltpu.HBM)
-    in_specs = [smem] * 3 + [hbm] * len(fetched)
+    in_specs = [smem] * 2 + [hbm] * len(fetched)
     scratch = [
         pltpu.VMEM((PARTS, cap, BS, 2 * CH), BF16),
         pltpu.VMEM((2, cols, BS, 2 * PANEL), BF16),
@@ -448,6 +461,7 @@
         pltpu.VMEM((3, 2 * PANEL, 2 * PANEL), BF16),
         pltpu.VMEM((2 * PANEL, 2 * PANEL), BF16),
         *[pltpu.VMEM(array.shape, BF16) for array in fetched],
+        pltpu.SMEM((PER * cols,), jnp.int32),
         pltpu.SemaphoreType.DMA((len(fetched),)),
         pltpu.SemaphoreType.DMA((2, cols)),
         pltpu.SemaphoreType.DMA((2, cols)),
@@ -484,6 +498,7 @@
     )(*operands)
     if fused:
         return result
+    place = plan(owner_of, rows, cols, cap)
     lidx, widx = pick_indices(place, trail_rows, owner_of, rows, cols)
     return pl.pallas_call(
         pick_body,

time: 114 us -> 109 us (0.956)
  Pallas kernels: 109 us -> 106 us
  other arithmetic: 1.45 us -> 0 us
    pallas_call x1, Pallas kernels: 109 us -> 106 us  [local(): pl.pallas_call(functools.partial(body, (rows, cols, cap, fill, width, fus...]
    add x1 -> x0, other arithmetic: 1.27 us -> none  [plan(): owners * cap + jnp.sum(same.astype(jnp.int32), axis=1, dtype=jnp.int32)]
where the time goes in v3:
time: 109 us; the launch traced here: 108 us
  Pallas kernels  106 us (97%)
  local copies, waits for them, and re-layouts  2.65 us (2%)
    pallas_call x1, Pallas kernels, local(): pl.pallas_call(functools.partial(body, (rows, cols, cap, fill, width, fus...  106 us
    unnamed x1, local copies, waits for them, and re-layouts  2.65 us

profile of v3, /device:TPU:1, one launch (start us, length us, event | category | flops | bytes accessed | tf_op | source)
XLA Modules:
  0.0 108.4 jit_solution(17657807723636766449)
XLA Ops:
  0.0 105.7 %shard_map.91 = bf16[256,3072]{1,0:T(8,128)(2,1)} custom-call(s32[192]{0:T(256)} %refs_0_.1, s32[4,24]{1,0:T(4,128)} %refs_1_.1, bf16[8,64,1024]{2,1,0:T(8,128)(2,1)} %bitcast.2, bf16[2,256,256]{2,1,0:T(8,128)(2,1)} %refs_3_.1, bf16[2,256,256]{2,1,0:T(8,128)(2,1)} %refs_4_.1, bf16[8,64,1024]{2,1,0:T(8,128)(2,1)} %bitcast.3, bf16[2,256,256]{2,1,0:T(8,128)(2,1)} %refs_6_.1, ...), custom_call_target="tpu_custom_call" | custom-call | tf_op jit(solution)/shard_map/pallas_call | solution.py:489
  105.7 2.7 %copy.11 = bf16[256,3072]{1,0:T(8,128)(2,1)} copy(bf16[256,3072]{1,0:T(8,128)(2,1)} %shard_map.91) | data formatting | bytes 3145728

commit v4 on v3

--- a/solution.py
+++ b/solution.py
@@ -54,8 +54,8 @@
     l_all, w_all = refs[:PARTS], refs[PARTS : PARTS + 2]
     refs = refs[PARTS + 2 :]
     if fused:
-        acc, trail_v, trail_sem = refs[:3]
-        refs = refs[3:]
+        acc, trail_v, trail_sem, out_v, out_sem = refs[:5]
+        refs = refs[5:]
     own_l, stage, w_low, rf, gt = refs[:5]
     held = refs[5:11]
     y_ref, cl, inv1, x_ref, cr, inv2 = held
@@ -329,6 +329,10 @@
 
     lax.fori_loop(0, n_tiles, second_l, 0)
 
+    def write_out(g):
+        lanes = pl.ds(g * PER * 2 * BS, PER * 2 * BS)
+        return pltpu.make_async_copy(out_v.at[:, lanes], out_ref.at[:, lanes], out_sem.at[g])
+
     def update(p):
         h = p // 2
 
@@ -346,10 +350,17 @@
             elif p < PARTS - 1:
                 acc[q] = acc[q] - change
             else:
-                out_ref[:, lanes] = (acc[q] - change).astype(BF16)
+                out_v[:, lanes] = (acc[q] - change).astype(BF16)
             return carry
 
-        lax.fori_loop(0, width, column, 0, unroll=4)
+        if p < PARTS - 1:
+            lax.fori_loop(0, width, column, 0, unroll=4)
+            return
+        for g in range(rows):
+            lax.fori_loop(g * PER, (g + 1) * PER, column, 0, unroll=PER)
+            write_out(g).start()
+        for g in range(rows):
+            write_out(g).wait()
 
     def finish(p):
         await_l(p)
@@ -450,7 +461,6 @@
     fetched = [owner_y.reshape(blocks), cl, inv1, owner_x.reshape(blocks), cr, inv2]
     operands = [owner_of, trail_rows] + fetched
     smem = pl.BlockSpec(memory_space=pltpu.SMEM)
-    vmem = pl.BlockSpec(memory_space=pltpu.VMEM)
     anywhere = pl.BlockSpec(memory_space=pl.ANY)
     hbm = pl.BlockSpec(memory_space=pltpu.HBM)
     in_specs = [smem] * 2 + [hbm] * len(fetched)
@@ -476,11 +486,13 @@
         operands.append(trail)
         in_specs.append(hbm)
         out_shape = jax.ShapeDtypeStruct(trail.shape, BF16)
-        out_specs = vmem
+        out_specs = hbm
         scratch = [pltpu.VMEM(l_shape, BF16)] * PARTS + [pltpu.VMEM(w_shape, BF16)] * 2 + [
             pltpu.VMEM((width, fill * BS, 2 * BS), F32),
             pltpu.VMEM(trail.shape, BF16),
             pltpu.SemaphoreType.DMA,
+            pltpu.VMEM(trail.shape, BF16),
+            pltpu.SemaphoreType.DMA((rows,)),
         ] + scratch
     else:
         out_shape = [jax.ShapeDtypeStruct(l_shape, BF16)] * PARTS

time: 109 us -> 107 us (0.982)
  Pallas kernels: 106 us -> 104 us
    pallas_call x1, Pallas kernels: 106 us -> 104 us  [local(): pl.pallas_call(functools.partial(body, (rows, cols, cap, fill, width, fus...]
where the time goes in v4:
time: 107 us
  Pallas kernels  104 us (97%)
  local copies, waits for them, and re-layouts  2.65 us (2%)
    pallas_call x1, Pallas kernels, local(): pl.pallas_call(functools.partial(body, (rows, cols, cap, fill, width, fus...  104 us
    unnamed x1, local copies, waits for them, and re-layouts  2.65 us

profile of v4, /device:TPU:1, one launch (start us, length us, event | category | flops | bytes accessed | tf_op | source)
XLA Modules:
  0.0 107.0 jit_solution(15290124589499042901)
XLA Ops:
  0.0 104.4 %shard_map.91 = bf16[256,3072]{1,0:T(8,128)(2,1)} custom-call(s32[192]{0:T(256)} %refs_0_.1, s32[4,24]{1,0:T(4,128)} %refs_1_.1, bf16[8,64,1024]{2,1,0:T(8,128)(2,1)} %bitcast.2, bf16[2,256,256]{2,1,0:T(8,128)(2,1)} %refs_3_.1, bf16[2,256,256]{2,1,0:T(8,128)(2,1)} %refs_4_.1, bf16[8,64,1024]{2,1,0:T(8,128)(2,1)} %bitcast.3, bf16[2,256,256]{2,1,0:T(8,128)(2,1)} %refs_6_.1, ...), custom_call_target="tpu_custom_call" | custom-call | tf_op jit(solution)/shard_map/pallas_call | solution.py:501
  104.4 2.7 %copy.11 = bf16[256,3072]{1,0:T(8,128)(2,1)} copy(bf16[256,3072]{1,0:T(8,128)(2,1)} %shard_map.91) | data formatting | bytes 3145728
